TPU v7x, 32 devices: a whole 2x2x4 slice. The times are simulated.
32 devices in a mesh: dom: 16 (over z, x, core), feat: 2 (over y).
Axes of the slice: x: 2, y: 2, z: 4, core: 2. Of those that a mesh axis runs over, the one named last changes fastest.
Arguments:
- fine_latent: bfloat16 [256, 262144], P('feat', 'dom'), may hold values from -6 to 6
- coarse_latent: bfloat16 [256, 131072], P('feat', 'dom'), may hold values from -6 to 6
- parents: int32 [4, 262144], P(None, 'dom'), may hold values from 0 to 24575, as said below
- interp_weights: float32 [4, 262144], P(None, 'dom'), may hold values from 0.1 to 1
- live_rows: int32 [16], P('dom'), may hold values from 8192 to 16384, as said below
- w_fine: bfloat16 [256, 256], replicated, may hold values from -0.25 to 0.25
- w_parent: bfloat16 [256, 256], replicated, may hold values from -0.25 to 0.25
- w_edge_out: bfloat16 [256, 256], replicated, may hold values from -0.375 to 0.375
- w_node_fine: bfloat16 [256, 256], replicated, may hold values from -0.25 to 0.25
- w_node_agg: bfloat16 [256, 256], replicated, may hold values from -0.25 to 0.25
- w_node_out: bfloat16 [256, 256], replicated, may hold values from -0.375 to 0.375
- edge_bias: float32 [256], replicated, may hold values from -3 to 3
- node_bias: float32 [256], replicated, may hold values from -3 to 3
- norm_gain: float32 [256], replicated, may hold values from 0.1 to 1.9
- norm_bias: float32 [256], replicated, may hold values from -2 to 2
Outputs:
- fine_out: bfloat16 [256, 262144], P('feat', 'dom')
Inputs may be any that keep to these rules, and one draw needn't show every extreme that they name: `parents`: a parent slot s of a fine node of block b names coarse node (b - 1) * 8192 + s, block b holding coarse nodes b * 8192 to (b + 1) * 8192 - 1; slots of block 0 are at least 8192, slots of the last block under 2 * 8192. `live_rows`: fine node slots of a block at or beyond its count are padding; at least one block is full.
All inputs are finite; a program needn't handle non-finite values.
Results may differ from a plain program's by a relative error of at most 0.0042.
Values may be sent and summed in bfloat16 or wider, within the bound.
No kernel may reach another device: no remote copies, remote signals or barrier semaphores. Data moves between devices by JAX's collectives and lax.ppermute only.
A program may use at most 128 MiB of HBM per device.

v0:
```python
import functools

import jax
import jax.numpy as jnp
from jax import lax
from jax.experimental import pallas as pl
from jax.experimental.pallas import tpu as pltpu
from jax.sharding import PartitionSpec as P

F32 = jnp.float32
BF16 = jnp.bfloat16
PAD = 8
CHUNKS = 2
GROUPS = 16


def dot(a, b, ca, cb):
    return lax.dot_general(a, b, (((ca,), (cb,)), ((), ())), preferred_element_type=F32)


def table_kernel(count, step, *refs):
    pieces, (weight, table, landed, sems) = refs[:-4], refs[-4:]
    blocks = len(pieces) // count
    rows = pieces[0].shape[1]
    steps = rows // step
    table[pl.ds(0, PAD), :] = jnp.zeros((PAD, 128), F32)
    table[pl.ds(PAD + 2 * blocks * rows, PAD), :] = jnp.zeros((PAD, 128), F32)

    def copies(block, i, slot):
        at = pl.multiple_of(i * step, step)
        features = pieces[0].shape[0]
        return [
            pltpu.make_async_copy(
                pieces[block * count + p].at[:, pl.ds(at, step)],
                landed.at[block % 2, slot, pl.ds(p * features, features), :],
                sems.at[block % 2, slot, p],
            )
            for p in range(count)
        ]

    for copy in copies(0, 0, 0):
        copy.start()
    for block in range(blocks):
        if block + 1 < blocks:
            for copy in copies(block + 1, 0, 0):
                copy.start()

        def one(i, carry, block=block):
            slot = lax.rem(i, 2)

            @pl.when(i + 1 < steps)
            def _():
                for copy in copies(block, i + 1, 1 - slot):
                    copy.start()

            for copy in copies(block, i, slot):
                copy.wait()
            projected = dot(landed[block % 2, slot], weight[...], 0, 0)
            base = pl.multiple_of(PAD + 2 * (block * rows + i * step), 8)
            table[pl.ds(base, step, stride=2), :] = projected[:, :128]
            table[pl.ds(base + 1, step, stride=2), :] = projected[:, 128:]
            return carry

        lax.fori_loop(0, steps, one, 0)


def update_kernel(count, step, live, slots, *refs):
    pieces = refs[:count]
    table, scales, w_latent, w_edge, w_agg, w_out_t, bias, gain, shift = refs[count : count + 9]
    outs = refs[count + 9 : 2 * count + 9]
    fine, total, spread_out, scale_rows = refs[2 * count + 9 :]
    parents = slots.shape[0]
    nodes = pieces[0].shape[1]
    sublane = lax.broadcasted_iota(jnp.int32, (8, 128), 0)
    owns = [sublane >= 2 * j for j in range(4)]

    def one_step(i, carry):
        at = pl.multiple_of(i * step, step)
        latent = jnp.concatenate([piece[:, pl.ds(at, step)] for piece in pieces], axis=0)
        first = dot(latent, w_latent[...], 0, 0) + bias[...]
        width = first.shape[1] // 2
        scale_rows[...] = scales[:, pl.ds(pl.multiple_of(2 * at, 2 * step), 2 * step)].T
        fine[pl.ds(0, step, stride=2), :] = first[:, :128]
        fine[pl.ds(1, step, stride=2), :] = first[:, 128:width]
        spread_out[...] = first[:, width:]

        def group(g):
            base = pl.multiple_of(g * 8, 8)
            node = at + g * 4
            part = fine[pl.ds(base, 8), :]
            scale = scale_rows[pl.ds(base, 8), :]
            acc = None
            for k in range(parents):
                rows = None
                for j in range(4):
                    loaded = table[pl.ds(slots[k, node + j] + (PAD - 2 * j), 8), :]
                    rows = loaded if rows is None else jnp.where(owns[j], loaded, rows)
                hidden = jnp.maximum(part + rows, 0.0) * scale[:, k : k + 1]
                acc = hidden if acc is None else acc + hidden
            return acc

        def some_groups(b, inner):
            sums = [group(b * GROUPS + u) for u in range(GROUPS)]
            total[pl.ds(pl.multiple_of(b * GROUPS * 8, 8), GROUPS * 8), :] = jnp.concatenate(sums, axis=0)
            return inner

        lax.fori_loop(0, step // (4 * GROUPS), some_groups, 0)
        summed = jnp.concatenate(
            [total[pl.ds(0, step, stride=2), :], total[pl.ds(1, step, stride=2), :]], axis=1
        ).astype(BF16)
        aggregate = dot(summed, w_edge[...], 1, 0).astype(BF16)
        node_hidden = jnp.maximum(spread_out[...] + dot(aggregate, w_agg[...], 1, 0), 0.0).astype(BF16)
        output = dot(w_out_t[...], node_hidden, 1, 1)
        centered = output - jnp.mean(output, axis=0, keepdims=True)
        spread = jnp.mean(centered * centered, axis=0, keepdims=True)
        normed = centered * lax.rsqrt(spread + 1e-05) * gain[...] + shift[...]
        column = at + lax.broadcasted_iota(jnp.int32, (1, step), 1)
        moved = jnp.where(column < live[0], normed, 0.0)
        result = (latent.astype(F32) + moved).astype(BF16)
        part_rows = result.shape[0] // count
        for r in range(count):
            outs[r][:, pl.ds(at, step)] = result[r * part_rows : (r + 1) * part_rows]
        return carry

    lax.fori_loop(0, nodes // step, one_step, 0)


def build_table(pieces, weight, count):
    rows = pieces[0].shape[1] * len(pieces) // count
    step = min(2048, pieces[0].shape[1])
    vmem = pl.BlockSpec(memory_space=pltpu.VMEM)
    return pl.pallas_call(
        functools.partial(table_kernel, count, step),
        out_shape=jax.ShapeDtypeStruct((2 * rows + 2 * PAD, 128), F32),
        in_specs=[pl.BlockSpec(memory_space=pl.ANY)] * len(pieces) + [vmem],
        out_specs=vmem,
        scratch_shapes=[
            pltpu.VMEM((2, 2, weight.shape[0], step), BF16),
            pltpu.SemaphoreType.DMA((2, 2, count)),
        ],
        compiler_params=pltpu.CompilerParams(vmem_limit_bytes=10 << 20),
        cost_estimate=pl.CostEstimate(flops=2 * rows * 65536, bytes_accessed=rows * 1536, transcendentals=0),
    )(*pieces, weight)


def update(live, slots, pieces, table, scales, params):
    count, nodes = len(pieces), pieces[0].shape[1]
    step = min(512, nodes)
    vmem = pl.BlockSpec(memory_space=pltpu.VMEM)
    smem = pl.BlockSpec(memory_space=pltpu.SMEM)
    return pl.pallas_call(
        functools.partial(update_kernel, count, step),
        out_shape=[jax.ShapeDtypeStruct(piece.shape, BF16) for piece in pieces],
        in_specs=[smem] * 2 + [vmem] * (count + 2 + len(params)),
        out_specs=[vmem] * count,
        scratch_shapes=[
            pltpu.VMEM((2 * step, 128), F32),
            pltpu.VMEM((2 * step, 128), F32),
            pltpu.VMEM((step, 256), F32),
            pltpu.VMEM((2 * step, 8), F32),
        ],
        compiler_params=pltpu.CompilerParams(vmem_limit_bytes=10 << 20),
        cost_estimate=pl.CostEstimate(flops=nodes * 700000, bytes_accessed=nodes * 2048, transcendentals=nodes),
    )(live, slots, *pieces, table, scales, *params)


def shards(
    fine_latent,
    coarse_latent,
    parents,
    interp_weights,
    live_rows,
    w_fine,
    w_parent,
    w_edge_out,
    w_node_fine,
    w_node_agg,
    w_node_out,
    edge_bias,
    node_bias,
    norm_gain,
    norm_bias,
):
    groups, domains = lax.axis_size("feat"), lax.axis_size("dom")
    rank = lax.axis_index("feat")
    own_features = fine_latent.shape[0]
    per_device = fine_latent.shape[1] // groups
    length = per_device // CHUNKS
    forward = [(i, i + 1) for i in range(domains - 1)]
    backward = [(i + 1, i) for i in range(domains - 1)]

    def turn(value, r):
        return lax.ppermute(value, "feat", [(i, (i + r) % groups) for i in range(groups)])

    owners = [(rank - r) % groups for r in range(groups)]
    own_block = [coarse_latent] + [turn(coarse_latent, r) for r in range(1, groups)]
    low = [lax.ppermute(piece, "dom", forward) for piece in own_block]
    high = [lax.ppermute(piece, "dom", backward) for piece in own_block]

    def ordered(weight, axis):
        parts = [lax.dynamic_slice_in_dim(weight, o * own_features, own_features, axis) for o in owners]
        return jnp.concatenate(parts, axis=axis)

    first_row = rank * per_device
    chunk_pieces = []
    for c in range(CHUNKS):
        pieces = [lax.dynamic_slice_in_dim(fine_latent, first_row + c * length, length, 1)]
        for r in range(1, groups):
            at = ((rank + r) % groups) * per_device + c * length
            part = lax.dynamic_slice_in_dim(fine_latent, at, length, 1)
            part, _ = lax.optimization_barrier((part, own_block[-1]))
            pieces.append(turn(part, r))
        chunk_pieces.append(pieces)

    table = build_table(low + own_block + high, ordered(w_parent, 0), groups)
    params = (
        jnp.concatenate([ordered(w_fine, 0), ordered(w_node_fine, 0)], axis=1),
        w_edge_out,
        w_node_agg,
        ordered(w_node_out, 1).T,
        jnp.concatenate([edge_bias, node_bias])[None],
        ordered(norm_gain, 0)[:, None],
        ordered(norm_bias, 0)[:, None],
    )
    slots = 2 * lax.dynamic_slice_in_dim(parents, first_row, per_device, 1)
    weights = lax.dynamic_slice_in_dim(interp_weights, first_row, per_device, 1)
    scales = jnp.pad(jnp.repeat(weights, 2, axis=1), ((0, 8 - weights.shape[0]), (0, 0)))
    result = fine_latent
    arrived = []
    for c in range(CHUNKS):
        start = c * length
        outs = update(
            live_rows - first_row - start,
            slots[:, start : start + length],
            chunk_pieces[c],
            table,
            scales[:, 2 * start : 2 * (start + length)],
            params,
        )
        result = lax.dynamic_update_slice_in_dim(result, outs[0], first_row + start, 1)
        for r in range(1, groups):
            arrived.append((turn(outs[r], -r), ((rank + r) % groups) * per_device + start))
    for part, at in arrived:
        result = lax.dynamic_update_slice_in_dim(result, part, at, 1)
    return result


def solution(mesh):
    in_specs = (P("feat", "dom"), P("feat", "dom"), P(None, "dom"), P(None, "dom"), P("dom")) + (P(),) * 10
    return jax.shard_map(shards, mesh=mesh, in_specs=in_specs, out_specs=P("feat", "dom"), check_vma=False)
```

profile of v0, /device:TPU:1, one launch (start us, length us, event | category | flops | bytes accessed | tf_op | source)
XLA Modules:
  0.0 249.7 jit_solution(17193320523888399488)
XLA Ops:
  0.0 0.0 copy-start
  0.0 0.0 copy-start.15
  0.0 0.0 copy-start.22
  0.0 0.0 copy-start.21
  0.0 0.0 copy-start.20
  0.1 0.0 copy-start.19
  0.1 4.7 %copy.34 = bf16[128,16384]{1,0:T(8,128)(2,1)} copy(bf16[128,16384]{1,0:T(8,128)(2,1)} %param.15) | data formatting | bytes 8388608
  4.8 4.6 %collective-permute-start.2 = (bf16[128,8192]{1,0:T(8,128)(2,1)S(1)}, bf16[128,8192]{1,0:T(8,128)(2,1)}, u32[]{:S(2)}, u32[]{:S(2)}) collective-permute-start(bf16[128,8192]{1,0:T(8,128)(2,1)S(1)} %copy-done.5), channel_id=1, source_target_pairs={{0,2},{2,4},{4,6},{6,8},{8,10},{10,12},{12,14},{14,16},{16,18},{18... | collective-permute-start | bytes 6291464 | tf_op jit(solution)/shard_map/ppermute | solution.py:197
  9.4 1.3 collective-permute-start
  10.7 2.2 collective-permute-start.4
  13.0 0.1 copy.26
  13.2 0.1 copy.27
  13.3 0.1 fusion.1
  13.4 3.1 %constant_dynamic-slice_fusion.11 = (bf16[128,4096]{1,0:T(8,128)(2,1)}, bf16[128,4096]{1,0:T(8,128)(2,1)}) fusion(bf16[128,16384]{1,0:T(8,128)(2,1)} %copy.34, s32[]{:T(128)S(6)} %select_n.57, s32[]{:T(128)S(6)} %select_n.55), kind=kLoop, calls=%fused_computation.21 | loop fusion | bytes 4194312 | tf_op jit(solution)/shard_map/dynamic_slice | solution.py:210
  16.5 0.7 pad_maximum_fusion.refs_6_
  17.2 0.0 copy-done.18
  17.3 39.9 %collective-permute-done.refs_3_ = bf16[128,8192]{1,0:T(8,128)(2,1)} collective-permute-done((bf16[128,8192]{1,0:T(8,128)(2,1)S(1)}, bf16[128,8192]{1,0:T(8,128)(2,1)}, u32[]{:S(2)}, u32[]{:S(2)}) %collective-permute-start) | collective-permute-done | bytes 2097184 | tf_op jit(solution)/shard_map/ppermute | solution.py:193
  57.2 2.3 collective-permute-start.5
  59.5 3.3 %collective-permute-start.3 = (bf16[128,8192]{1,0:T(8,128)(2,1)}, bf16[128,8192]{1,0:T(8,128)(2,1)}, u32[]{:S(2)}, u32[]{:S(2)}) collective-permute-start(bf16[128,8192]{1,0:T(8,128)(2,1)} %collective-permute-done.refs_3_), channel_id=1, source_target_pairs={{0,2},{2,4},{4,6},{6,8},{8,10},{10,12},{12,14},{14,16},{16,18},{18... | collective-permute-start | bytes 6291464 | tf_op jit(solution)/shard_map/ppermute | solution.py:197
  63.4 0.1 copy.22.refs_9_
  63.5 0.1 copy.23.refs_10_
  63.7 2.7 %copy.18 = f32[4,8192]{0,1:T(8,128)} copy(f32[4,8192]{1,0:T(4,128)S(1)} %constant_dynamic-slice_fusion.8) | data formatting | bytes 262144 | tf_op jit(solution)/shard_map/dynamic_slice | solution.py:226
  66.4 6.7 %broadcast_in_dim.12 = f32[4,8192,2]{0,2,1:T(2,128)} broadcast(f32[4,8192]{0,1:T(8,128)} %copy.18), dimensions={0,1} | broadcast | bytes 393216 | tf_op jit(solution)/shard_map/broadcast_in_dim | solution.py:227
  73.1 5.5 %copy.19 = f32[4,16384]{1,0:T(4,128)S(1)} copy(f32[4,16384]{0,1:T(8,128)} %bitcast.9) | data formatting | bytes 524288 | tf_op jit(solution)/shard_map/reshape | solution.py:227
  78.7 1.0 collective-permute-start.1
  79.7 0.0 collective-permute-done.2.refs_0_
  79.7 0.0 collective-permute-done.4.refs_4_
  79.7 5.3 %collective-permute-done.5.refs_5_ = bf16[128,8192]{1,0:T(8,128)(2,1)} collective-permute-done((bf16[128,8192]{1,0:T(8,128)(2,1)}, bf16[128,8192]{1,0:T(8,128)(2,1)}, u32[]{:S(2)}, u32[]{:S(2)}) %collective-permute-start.5) | collective-permute-done | bytes 2097184 | tf_op jit(solution)/shard_map/ppermute | solution.py:198
  85.0 21.6 %collective-permute-done.3.refs_1_ = bf16[128,8192]{1,0:T(8,128)(2,1)} collective-permute-done((bf16[128,8192]{1,0:T(8,128)(2,1)}, bf16[128,8192]{1,0:T(8,128)(2,1)}, u32[]{:S(2)}, u32[]{:S(2)}) %collective-permute-start.3) | collective-permute-done | bytes 2097184 | tf_op jit(solution)/shard_map/ppermute | solution.py:197
  106.7 1.6 copy-done.6
  108.3 0.9 copy-done.11
  109.2 10.8 %shard_map.145.refs_2_ = f32[49168,128]{1,0:T(8,128)S(1)} custom-call(bf16[128,8192]{1,0:T(8,128)(2,1)} %collective-permute-done.2.refs_0_, bf16[128,8192]{1,0:T(8,128)(2,1)} %collective-permute-done.3.refs_1_, bf16[128,8192]{1,0:T(8,128)(2,1)S(1)} %copy-done.6, bf16[128,8192]{1,0:T(8,128)(2,1)} %collective-permute-done.refs_3_, ...), custom_call_target="tpu_custom_call" | custom-call | flops 3221225472 | bytes 37748736 | tf_op jit(solution)/shard_map/pallas_call | solution.py:132
  120.0 0.0 collective-permute-done.1.refs_1_
  120.0 0.0 copy-start.12
  120.0 43.1 %shard_map.146 = (bf16[128,4096]{1,0:T(8,128)(2,1)S(1)}, bf16[128,4096]{1,0:T(8,128)(2,1)}) custom-call(s32[1]{0:T(128)S(6)} %sub.15.live, s32[4,4096]{1,0:T(4,128)S(1)} %get-tuple-element.25.slots, bf16[128,4096]{1,0:T(8,128)(2,1)S(1)} %copy-done.4, bf16[128,4096]{1,0:T(8,128)(2,1)S(1)} %collective-permute-done.1.refs_1_, ...), custom_call_target="tpu_custom_call" | custom-call | flops 2867200000 | bytes 8388608 | tf_op jit(solution)/shard_map/pallas_call | solution.py:151
  163.2 0.3 constant_dynamic-slice_fusion
  163.5 1.3 collective-permute-start.6
  164.8 0.2 collective-permute-start.7
  165.0 19.6 %collective-permute-done.6.refs_1_ = bf16[128,4096]{1,0:T(8,128)(2,1)S(1)} collective-permute-done((bf16[128,4096]{1,0:T(8,128)(2,1)S(1)}, bf16[128,4096]{1,0:T(8,128)(2,1)S(1)}, u32[]{:S(2)}, u32[]{:S(2)}) %collective-permute-start.6) | collective-permute-done | bytes 1048608 | tf_op jit(solution)/shard_map/ppermute | solution.py:193
  184.7 8.2 %copy-done.3 = f32[49168,128]{1,0:T(8,128)S(1)} copy-done((f32[49168,128]{1,0:T(8,128)S(1)}, f32[49168,128]{1,0:T(8,128)}, u32[]{:S(2)}) %copy-start.3) | copy-done | bytes 25174040
  192.8 42.1 %shard_map.147 = (bf16[128,4096]{1,0:T(8,128)(2,1)S(1)}, bf16[128,4096]{1,0:T(8,128)(2,1)S(1)}) custom-call(s32[1]{0:T(128)S(6)} %sub.17.live, s32[4,4096]{1,0:T(4,128)S(1)} %get-tuple-element.24.slots, bf16[128,4096]{1,0:T(8,128)(2,1)S(1)} %get-tuple-element.19.refs_0_, bf16[128,4096]{1,0:T(8,128)(2,1)S(1)} %collective-permute-done.6.refs_1_, ...), custom_call_target="tpu_custom_call" | custom-call | flops 2867200000 | bytes 8388608 | tf_op jit(solution)/shard_map/pallas_call | solution.py:151
  235.0 1.0 collective-permute-start.8
  236.0 0.1 constant_dynamic-update-slice_fusion.2
  236.1 0.0 collective-permute-done.7
  236.1 0.1 constant_dynamic-update-slice_fusion.1
  236.2 0.0 copy-start.13
  236.2 12.5 %collective-permute-done.8 = bf16[128,4096]{1,0:T(8,128)(2,1)S(1)} collective-permute-done((bf16[128,4096]{1,0:T(8,128)(2,1)S(1)}, bf16[128,4096]{1,0:T(8,128)(2,1)S(1)}, u32[]{:S(2)}, u32[]{:S(2)}) %collective-permute-start.8) | collective-permute-done | bytes 1048608 | tf_op jit(solution)/shard_map/ppermute | solution.py:193
  248.7 1.0 constant_dynamic-update-slice_fusion
  (46 shorter events, 0.3 us)
Async XLA Ops:
  0.0 17.3 %copy-start = (f32[4,16384]{1,0:T(4,128)S(1)}, f32[4,16384]{1,0:T(4,128)}, u32[]{:S(2)}) copy-start(f32[4,16384]{1,0:T(4,128)} %param.18) | copy-start | bytes 786436
  0.0 4.8 %copy-start.5 = (bf16[128,8192]{1,0:T(8,128)(2,1)S(1)}, bf16[128,8192]{1,0:T(8,128)(2,1)}, u32[]{:S(2)}) copy-start(bf16[128,8192]{1,0:T(8,128)(2,1)} %refs_2_.1) | copy-start | bytes 6291460
  0.0 13.0 %copy-start.14 = (bf16[256,256]{1,0:T(8,128)(2,1)S(1)}, bf16[256,256]{1,0:T(8,128)(2,1)}, u32[]{:S(2)}) copy-start(bf16[256,256]{1,0:T(8,128)(2,1)} %param.21) | copy-start | bytes 393220
  0.0 13.0 %copy-start.15 = (bf16[256,256]{1,0:T(8,128)(2,1)S(1)}, bf16[256,256]{1,0:T(8,128)(2,1)}, u32[]{:S(2)}) copy-start(bf16[256,256]{1,0:T(8,128)(2,1)} %param.25) | copy-start | bytes 393220
  0.0 13.3 %copy-start.22 = (f32[256]{0:T(256)S(1)}, f32[256]{0:T(256)}, u32[]{:S(2)}) copy-start(f32[256]{0:T(256)} %param.26) | copy-start | bytes 3076
  0.0 13.3 %copy-start.21 = (f32[256]{0:T(256)S(1)}, f32[256]{0:T(256)}, u32[]{:S(2)}) copy-start(f32[256]{0:T(256)} %param.27) | copy-start | bytes 3076
  0.0 13.3 %copy-start.20 = (f32[256]{0:T(256)S(1)}, f32[256]{0:T(256)}, u32[]{:S(2)}) copy-start(f32[256]{0:T(256)} %param.28) | copy-start | bytes 3076
  0.1 13.3 %copy-start.19 = (f32[256]{0:T(256)S(1)}, f32[256]{0:T(256)}, u32[]{:S(2)}) copy-start(f32[256]{0:T(256)} %param.29) | copy-start | bytes 3076
  4.8 12.4 %copy-start.18 = (s32[4,16384]{1,0:T(4,128)S(1)}, s32[4,16384]{1,0:T(4,128)}, u32[]{:S(2)}) copy-start(s32[4,16384]{1,0:T(4,128)} %param.17) | copy-start | bytes 786436
  4.8 74.9 %collective-permute-start.2 = (bf16[128,8192]{1,0:T(8,128)(2,1)S(1)}, bf16[128,8192]{1,0:T(8,128)(2,1)}, u32[]{:S(2)}, u32[]{:S(2)}) collective-permute-start(bf16[128,8192]{1,0:T(8,128)(2,1)S(1)} %copy-done.5), channel_id=1, source_target_pairs={{0,2},{2,4},{4,6},{6,8},{8,10},{10,12},{12,14},{14,16},{16,18},{18... | collective-permute-start | bytes 6291464 | tf_op jit(solution)/shard_map/ppermute | solution.py:197
  9.4 47.7 %collective-permute-start = (bf16[128,8192]{1,0:T(8,128)(2,1)S(1)}, bf16[128,8192]{1,0:T(8,128)(2,1)}, u32[]{:S(2)}, u32[]{:S(2)}) collective-permute-start(bf16[128,8192]{1,0:T(8,128)(2,1)S(1)} %copy-done.5), channel_id=1, source_target_pairs={{0,1},{1,0},{2,3},{3,2},{4,5},{5,4},{6,7},{7,6},{8,9},{9,8},{10,11... | collective-permute-start | bytes 6291464 | tf_op jit(solution)/shard_map/ppermute | solution.py:193
  10.7 69.0 %collective-permute-start.4 = (bf16[128,8192]{1,0:T(8,128)(2,1)S(1)}, bf16[128,8192]{1,0:T(8,128)(2,1)}, u32[]{:S(2)}, u32[]{:S(2)}) collective-permute-start(bf16[128,8192]{1,0:T(8,128)(2,1)S(1)} %copy-done.5), channel_id=1, source_target_pairs={{2,0},{4,2},{6,4},{8,6},{10,8},{12,10},{14,12},{16,14},{18,16},{20... | collective-permute-start | bytes 6291464 | tf_op jit(solution)/shard_map/ppermute | solution.py:198
  57.2 27.8 %collective-permute-start.5 = (bf16[128,8192]{1,0:T(8,128)(2,1)}, bf16[128,8192]{1,0:T(8,128)(2,1)}, u32[]{:S(2)}, u32[]{:S(2)}) collective-permute-start(bf16[128,8192]{1,0:T(8,128)(2,1)} %collective-permute-done.refs_3_), channel_id=1, source_target_pairs={{2,0},{4,2},{6,4},{8,6},{10,8},{12,10},{14,12},{16,14},{18,16},{20... | collective-permute-start | bytes 6291464 | tf_op jit(solution)/shard_map/ppermute | solution.py:198
  59.5 47.2 %collective-permute-start.3 = (bf16[128,8192]{1,0:T(8,128)(2,1)}, bf16[128,8192]{1,0:T(8,128)(2,1)}, u32[]{:S(2)}, u32[]{:S(2)}) collective-permute-start(bf16[128,8192]{1,0:T(8,128)(2,1)} %collective-permute-done.refs_3_), channel_id=1, source_target_pairs={{0,2},{2,4},{4,6},{6,8},{8,10},{10,12},{12,14},{14,16},{16,18},{18... | collective-permute-start | bytes 6291464 | tf_op jit(solution)/shard_map/ppermute | solution.py:197
  73.1 5.5 %copy-start.16 = (bf16[256,256]{1,0:T(8,128)(2,1)S(1)}, bf16[256,256]{1,0:T(8,128)(2,1)}, u32[]{:S(2)}) copy-start(bf16[256,256]{1,0:T(8,128)(2,1)} %param.23) | copy-start | bytes 393220
  73.1 5.5 %copy-start.17 = (bf16[256,256]{1,0:T(8,128)(2,1)S(1)}, bf16[256,256]{1,0:T(8,128)(2,1)}, u32[]{:S(2)}) copy-start(bf16[256,256]{1,0:T(8,128)(2,1)} %param.20) | copy-start | bytes 393220
  78.7 41.3 %collective-permute-start.1 = (bf16[128,4096]{1,0:T(8,128)(2,1)}, bf16[128,4096]{1,0:T(8,128)(2,1)S(1)}, u32[]{:S(2)}, u32[]{:S(2)}) collective-permute-start(bf16[128,4096]{1,0:T(8,128)(2,1)} %get-tuple-element.11), channel_id=1, source_target_pairs={{0,1},{1,0},{2,3},{3,2},{4,5},{5,4},{6,7},{7,6},{8,9},{9,8},{10,11... | collective-permute-start | bytes 3145736 | tf_op jit(solution)/shard_map/ppermute | solution.py:193
  79.7 40.3 %copy-start.7 = (bf16[256,256]{1,0:T(8,128)(2,1)S(1)}, bf16[256,256]{1,0:T(8,128)(2,1)}, u32[]{:S(2)}) copy-start(bf16[256,256]{1,0:T(8,128)(2,1)} %refs_5_.3) | copy-start | bytes 393220
  79.7 40.3 %copy-start.9 = (bf16[256,256]{1,0:T(8,128)(2,1)S(1)}, bf16[256,256]{1,0:T(8,128)(2,1)}, u32[]{:S(2)}) copy-start(bf16[256,256]{1,0:T(8,128)(2,1)} %refs_6_.3) | copy-start | bytes 393220
  79.7 40.3 %copy-start.4 = (bf16[128,4096]{1,0:T(8,128)(2,1)S(1)}, bf16[128,4096]{1,0:T(8,128)(2,1)}, u32[]{:S(2)}) copy-start(bf16[128,4096]{1,0:T(8,128)(2,1)} %get-tuple-element.21.refs_0_) | copy-start | bytes 3145732
  106.7 1.6 copy-start.6
  108.3 0.9 copy-start.11
  120.0 43.2 %copy-start.2 = (f32[49168,128]{1,0:T(8,128)}, f32[49168,128]{1,0:T(8,128)S(1)}, u32[]{:S(2)}) copy-start(f32[49168,128]{1,0:T(8,128)S(1)} %shard_map.145.refs_2_) | copy-start | bytes 75522048
  120.0 43.1 %copy-start.12 = (bf16[128,16384]{1,0:T(8,128)(2,1)S(1)}, bf16[128,16384]{1,0:T(8,128)(2,1)}, u32[]{:S(2)}) copy-start(bf16[128,16384]{1,0:T(8,128)(2,1)} %copy.34) | copy-start | bytes 12582916
  163.2 21.5 %copy-start.8 = (bf16[256,256]{1,0:T(8,128)(2,1)S(1)}, bf16[256,256]{1,0:T(8,128)(2,1)}, u32[]{:S(2)}) copy-start(bf16[256,256]{1,0:T(8,128)(2,1)} %refs_5_.3) | copy-start | bytes 393220
  163.2 21.5 %copy-start.10 = (bf16[256,256]{1,0:T(8,128)(2,1)S(1)}, bf16[256,256]{1,0:T(8,128)(2,1)}, u32[]{:S(2)}) copy-start(bf16[256,256]{1,0:T(8,128)(2,1)} %refs_6_.3) | copy-start | bytes 393220
  163.5 21.2 %collective-permute-start.6 = (bf16[128,4096]{1,0:T(8,128)(2,1)S(1)}, bf16[128,4096]{1,0:T(8,128)(2,1)S(1)}, u32[]{:S(2)}, u32[]{:S(2)}) collective-permute-start(bf16[128,4096]{1,0:T(8,128)(2,1)S(1)} %get-tuple-element.13), channel_id=1, source_target_pairs={{0,1},{1,0},{2,3},{3,2},{4,5},{5,4},{6,7},{7,6},{8,9},{9,8},{10,11... | collective-permute-start | bytes 3145736 | tf_op jit(solution)/shard_map/ppermute | solution.py:193
  164.8 71.3 %collective-permute-start.7 = (bf16[128,4096]{1,0:T(8,128)(2,1)}, bf16[128,4096]{1,0:T(8,128)(2,1)S(1)}, u32[]{:S(2)}, u32[]{:S(2)}) collective-permute-start(bf16[128,4096]{1,0:T(8,128)(2,1)} %get-tuple-element.15), channel_id=1, source_target_pairs={{0,1},{1,0},{2,3},{3,2},{4,5},{5,4},{6,7},{7,6},{8,9},{9,8},{10,11... | collective-permute-start | bytes 3145736 | tf_op jit(solution)/shard_map/ppermute | solution.py:193
  184.7 8.2 %copy-start.3 = (f32[49168,128]{1,0:T(8,128)S(1)}, f32[49168,128]{1,0:T(8,128)}, u32[]{:S(2)}) copy-start(f32[49168,128]{1,0:T(8,128)} %copy-done.2) | copy-start | bytes 75522048
  192.8 56.9 %copy-start.1 = (f32[4,16384]{1,0:T(4,128)S(1)}, f32[4,16384]{1,0:T(4,128)}, u32[]{:S(2)}) copy-start(f32[4,16384]{1,0:T(4,128)} %param.18) | copy-start | bytes 786436
  235.0 13.7 %collective-permute-start.8 = (bf16[128,4096]{1,0:T(8,128)(2,1)S(1)}, bf16[128,4096]{1,0:T(8,128)(2,1)S(1)}, u32[]{:S(2)}, u32[]{:S(2)}) collective-permute-start(bf16[128,4096]{1,0:T(8,128)(2,1)S(1)} %get-tuple-element.16), channel_id=1, source_target_pairs={{0,1},{1,0},{2,3},{3,2},{4,5},{5,4},{6,7},{7,6},{8,9},{9,8},{10,11... | collective-permute-start | bytes 3145736 | tf_op jit(solution)/shard_map/ppermute | solution.py:193
  236.2 12.5 %copy-start.13 = (bf16[128,16384]{1,0:T(8,128)(2,1)}, bf16[128,16384]{1,0:T(8,128)(2,1)S(1)}, u32[]{:S(2)}) copy-start(bf16[128,16384]{1,0:T(8,128)(2,1)S(1)} %constant_dynamic-update-slice_fusion.1) | copy-start | bytes 12582916
where the time goes:
time: 250 us
  waiting for transfers between devices  98.9 us (40%)
  Pallas kernels  96.1 us (38%)
  local copies, waits for them, and re-layouts  35.7 us (14%)
  starting transfers between devices  17.2 us (7%)
    pallas_call x2, Pallas kernels, update(): pl.pallas_call(functools.partial(update_kernel, count, step), out_shape=[...  85.2 us
    ppermute x5, waiting for transfers between devices, turn(): lax.ppermute(value, 'feat', [(i, (i + r) % groups) for i in range(groups)])  72 us
    ppermute x2, waiting for transfers between devices, shards(): low = [lax.ppermute(piece, 'dom', forward) for piece in own_block]  21.7 us
    unnamed x49, local copies, waits for them, and re-layouts  15.7 us
    pallas_call x1, Pallas kernels, build_table(): pl.pallas_call(functools.partial(table_kernel, count, step), out_shape=ja...  10.8 us
    ppermute x2, starting transfers between devices, shards(): low = [lax.ppermute(piece, 'dom', forward) for piece in own_block]  7.89 us
    broadcast_in_dim x1, local copies, waits for them, and re-layouts, shards(): jnp.repeat(weights, 2, axis=1)  6.65 us
    reshape x1, local copies, waits for them, and re-layouts, shards(): jnp.repeat(weights, 2, axis=1)  5.49 us
  transfers between devices with their start and end apart: 9, of which 5 were waited for; matrix products, arithmetic and copies ran while one was open for 8% of the time, Pallas kernels for 21%

commit v1 on v0

--- a/solution.py
+++ b/solution.py
@@ -9,7 +9,7 @@
 
 F32 = jnp.float32
 BF16 = jnp.bfloat16
-PAD = 8
+PAD = 4
 CHUNKS = 2
 GROUPS = 16
 
@@ -23,8 +23,9 @@
     blocks = len(pieces) // count
     rows = pieces[0].shape[1]
     steps = rows // step
-    table[pl.ds(0, PAD), :] = jnp.zeros((PAD, 128), F32)
-    table[pl.ds(PAD + 2 * blocks * rows, PAD), :] = jnp.zeros((PAD, 128), F32)
+    flat = table.reshape(2 * table.shape[0], 128)
+    flat[pl.ds(0, 2 * PAD), :] = jnp.zeros((2 * PAD, 128), F32)
+    flat[pl.ds(2 * (PAD + blocks * rows), 2 * PAD), :] = jnp.zeros((2 * PAD, 128), F32)
 
     def copies(block, i, slot):
         at = pl.multiple_of(i * step, step)
@@ -56,9 +57,9 @@
             for copy in copies(block, i, slot):
                 copy.wait()
             projected = dot(landed[block % 2, slot], weight[...], 0, 0)
-            base = pl.multiple_of(PAD + 2 * (block * rows + i * step), 8)
-            table[pl.ds(base, step, stride=2), :] = projected[:, :128]
-            table[pl.ds(base + 1, step, stride=2), :] = projected[:, 128:]
+            base = pl.multiple_of(2 * (PAD + block * rows + i * step), 8)
+            flat[pl.ds(base, step, stride=2), :] = projected[:, :128]
+            flat[pl.ds(base + 1, step, stride=2), :] = projected[:, 128:]
             return carry
 
         lax.fori_loop(0, steps, one, 0)
@@ -93,7 +94,7 @@
             for k in range(parents):
                 rows = None
                 for j in range(4):
-                    loaded = table[pl.ds(slots[k, node + j] + (PAD - 2 * j), 8), :]
+                    loaded = table.at[pl.ds(slots[k, node + j] + (PAD - j), 4)].reshape(8, 128)[...]
                     rows = loaded if rows is None else jnp.where(owns[j], loaded, rows)
                 hidden = jnp.maximum(part + rows, 0.0) * scale[:, k : k + 1]
                 acc = hidden if acc is None else acc + hidden
@@ -131,7 +132,7 @@
     vmem = pl.BlockSpec(memory_space=pltpu.VMEM)
     return pl.pallas_call(
         functools.partial(table_kernel, count, step),
-        out_shape=jax.ShapeDtypeStruct((2 * rows + 2 * PAD, 128), F32),
+        out_shape=jax.ShapeDtypeStruct((rows + 2 * PAD, 2, 128), F32),
         in_specs=[pl.BlockSpec(memory_space=pl.ANY)] * len(pieces) + [vmem],
         out_specs=vmem,
         scratch_shapes=[
@@ -222,7 +223,7 @@
         ordered(norm_gain, 0)[:, None],
         ordered(norm_bias, 0)[:, None],
     )
-    slots = 2 * lax.dynamic_slice_in_dim(parents, first_row, per_device, 1)
+    slots = lax.dynamic_slice_in_dim(parents, first_row, per_device, 1)
     weights = lax.dynamic_slice_in_dim(interp_weights, first_row, per_device, 1)
     scales = jnp.pad(jnp.repeat(weights, 2, axis=1), ((0, 8 - weights.shape[0]), (0, 0)))
     result = fine_latent

time: 250 us -> 253 us (1.012)
  Pallas kernels: 96.1 us -> 105 us
  waiting for transfers between devices: 98.9 us -> 92.9 us
    pallas_call x2, Pallas kernels: 85.2 us -> 93.9 us  [update(): pl.pallas_call(functools.partial(update_kernel, count, step), out_shape=[...]
    ppermute x5, waiting for transfers between devices: 72 us -> 64.4 us  [turn(): lax.ppermute(value, 'feat', [(i, (i + r) % groups) for i in range(groups)])]
    unnamed x49 -> x47, local copies, waits for them, and re-layouts: 15.7 us -> 15.7 us
  transfers between devices with their start and end apart: 9 -> 9, of which waited for: 5 -> 5; matrix products, arithmetic and copies ran while one was open for 8% -> 7% of each run, Pallas kernels for 21% -> 23%
where the time goes in v1:
time: 253 us; the launch traced here: 252 us
  Pallas kernels  105 us (42%)
  waiting for transfers between devices  92.9 us (37%)
  local copies, waits for them, and re-layouts  34.4 us (14%)
  starting transfers between devices  18.5 us (7%)
    pallas_call x2, Pallas kernels, update(): pl.pallas_call(functools.partial(update_kernel, count, step), out_shape=[...  93.9 us
    ppermute x5, waiting for transfers between devices, turn(): lax.ppermute(value, 'feat', [(i, (i + r) % groups) for i in range(groups)])  64.4 us
    ppermute x2, waiting for transfers between devices, shards(): low = [lax.ppermute(piece, 'dom', forward) for piece in own_block]  21.6 us
    unnamed x47, local copies, waits for them, and re-layouts  15.7 us
    pallas_call x1, Pallas kernels, build_table(): pl.pallas_call(functools.partial(table_kernel, count, step), out_shape=ja...  10.8 us
    ppermute x2, starting transfers between devices, shards(): low = [lax.ppermute(piece, 'dom', forward) for piece in own_block]  7.19 us
    ppermute x2, waiting for transfers between devices, shards(): high = [lax.ppermute(piece, 'dom', backward) for piece in own_block]  6.86 us
    broadcast_in_dim x1, local copies, waits for them, and re-layouts, shards(): jnp.repeat(weights, 2, axis=1)  6.76 us
  transfers between devices with their start and end apart: 9, of which 5 were waited for; matrix products, arithmetic and copies ran while one was open for 7% of the time, Pallas kernels for 23%

profile of v1, /device:TPU:1, one launch (start us, length us, event | category | flops | bytes accessed | tf_op | source)
XLA Modules:
  0.0 252.3 jit_solution(6624838354154115136)
XLA Ops:
  0.0 0.0 copy-start
  0.0 0.0 copy-start.19
  0.0 4.7 %copy.34 = bf16[128,16384]{1,0:T(8,128)(2,1)} copy(bf16[128,16384]{1,0:T(8,128)(2,1)} %param.15) | data formatting | bytes 8388608
  4.8 0.0 copy-start.15
  4.8 0.0 copy-start.16
  4.8 2.1 collective-permute-start
  6.9 3.9 %collective-permute-start.2 = (bf16[128,8192]{1,0:T(8,128)(2,1)S(1)}, bf16[128,8192]{1,0:T(8,128)(2,1)}, u32[]{:S(2)}, u32[]{:S(2)}) collective-permute-start(bf16[128,8192]{1,0:T(8,128)(2,1)S(1)} %copy-done.4), channel_id=1, source_target_pairs={{0,2},{2,4},{4,6},{6,8},{8,10},{10,12},{12,14},{14,16},{16,18},{18... | collective-permute-start | bytes 6291464 | tf_op jit(solution)/shard_map/ppermute | solution.py:198
  10.9 1.9 collective-permute-start.4
  13.5 0.1 fusion
  13.6 0.1 copy.22.refs_9_
  13.8 0.1 copy.23.refs_10_
  14.0 0.1 copy.26
  14.1 0.1 copy.27
  14.2 2.7 %copy.18 = f32[4,8192]{0,1:T(8,128)} copy(f32[4,8192]{1,0:T(4,128)S(1)} %constant_dynamic-slice_fusion.9) | data formatting | bytes 262144 | tf_op jit(solution)/shard_map/dynamic_slice | solution.py:227
  16.9 0.0 copy-done.21
  17.0 0.7 pad_maximum_fusion.refs_6_
  17.7 34.7 %collective-permute-done.refs_3_ = bf16[128,8192]{1,0:T(8,128)(2,1)} collective-permute-done((bf16[128,8192]{1,0:T(8,128)(2,1)S(1)}, bf16[128,8192]{1,0:T(8,128)(2,1)}, u32[]{:S(2)}, u32[]{:S(2)}) %collective-permute-start) | collective-permute-done | bytes 2097184 | tf_op jit(solution)/shard_map/ppermute | solution.py:194
  52.4 3.1 %collective-permute-start.5 = (bf16[128,8192]{1,0:T(8,128)(2,1)}, bf16[128,8192]{1,0:T(8,128)(2,1)}, u32[]{:S(2)}, u32[]{:S(2)}) collective-permute-start(bf16[128,8192]{1,0:T(8,128)(2,1)} %collective-permute-done.refs_3_), channel_id=1, source_target_pairs={{2,0},{4,2},{6,4},{8,6},{10,8},{12,10},{14,12},{16,14},{18,16},{20... | collective-permute-start | bytes 6291464 | tf_op jit(solution)/shard_map/ppermute | solution.py:199
  55.5 3.2 %collective-permute-start.3 = (bf16[128,8192]{1,0:T(8,128)(2,1)}, bf16[128,8192]{1,0:T(8,128)(2,1)}, u32[]{:S(2)}, u32[]{:S(2)}) collective-permute-start(bf16[128,8192]{1,0:T(8,128)(2,1)} %collective-permute-done.refs_3_), channel_id=1, source_target_pairs={{0,2},{2,4},{4,6},{6,8},{8,10},{10,12},{12,14},{14,16},{16,18},{18... | collective-permute-start | bytes 6291464 | tf_op jit(solution)/shard_map/ppermute | solution.py:198
  58.8 6.8 %broadcast_in_dim.12 = f32[4,8192,2]{0,2,1:T(2,128)} broadcast(f32[4,8192]{0,1:T(8,128)} %copy.18), dimensions={0,1} | broadcast | bytes 393216 | tf_op jit(solution)/shard_map/broadcast_in_dim | solution.py:228
  65.5 5.5 %copy.19 = f32[4,16384]{1,0:T(4,128)S(1)} copy(f32[4,16384]{0,1:T(8,128)} %bitcast.9) | data formatting | bytes 524288 | tf_op jit(solution)/shard_map/reshape | solution.py:228
  71.1 1.7 constant_dynamic-slice_fusion.12
  72.8 1.3 collective-permute-start.1
  74.2 0.0 collective-permute-done.2.refs_0_
  74.2 0.0 collective-permute-done.4.refs_4_
  74.2 6.9 %collective-permute-done.5.refs_5_ = bf16[128,8192]{1,0:T(8,128)(2,1)} collective-permute-done((bf16[128,8192]{1,0:T(8,128)(2,1)}, bf16[128,8192]{1,0:T(8,128)(2,1)}, u32[]{:S(2)}, u32[]{:S(2)}) %collective-permute-start.5) | collective-permute-done | bytes 2097184 | tf_op jit(solution)/shard_map/ppermute | solution.py:199
  81.0 21.6 %collective-permute-done.3.refs_1_ = bf16[128,8192]{1,0:T(8,128)(2,1)} collective-permute-done((bf16[128,8192]{1,0:T(8,128)(2,1)}, bf16[128,8192]{1,0:T(8,128)(2,1)}, u32[]{:S(2)}, u32[]{:S(2)}) %collective-permute-start.3) | collective-permute-done | bytes 2097184 | tf_op jit(solution)/shard_map/ppermute | solution.py:198
  102.7 1.6 copy-done.5
  104.3 0.9 copy-done.10
  105.2 10.8 %shard_map.145.refs_2_ = f32[24584,2,128]{2,1,0:T(2,128)S(1)} custom-call(bf16[128,8192]{1,0:T(8,128)(2,1)} %collective-permute-done.2.refs_0_, bf16[128,8192]{1,0:T(8,128)(2,1)} %collective-permute-done.3.refs_1_, bf16[128,8192]{1,0:T(8,128)(2,1)S(1)} %copy-done.5, bf16[128,8192]{1,0:T(8,128)(2,1)} %collective-permute-done.refs_3_, ...), custom_call_target="tpu_custom_call" | custom-call | flops 3221225472 | bytes 37748736 | tf_op jit(solution)/shard_map/pallas_call | solution.py:133
  116.0 0.0 collective-permute-done.1.refs_1_
  116.0 0.0 copy-done.6
  116.1 0.0 copy-done.8
  116.1 0.0 copy-start.11
  116.1 47.5 %shard_map.146 = (bf16[128,4096]{1,0:T(8,128)(2,1)S(1)}, bf16[128,4096]{1,0:T(8,128)(2,1)}) custom-call(s32[1]{0:T(128)S(6)} %sub.15.live, s32[4,4096]{1,0:T(4,128)S(1)} %get-tuple-element.25.slots, bf16[128,4096]{1,0:T(8,128)(2,1)S(1)} %get-tuple-element.21.refs_0_, bf16[128,4096]{1,0:T(8,128)(2,1)S(1)} %collective-permute-done.1.refs_1_, ...), custom_call_target="tpu_custom_call" | custom-call | flops 2867200000 | bytes 8388608 | tf_op jit(solution)/shard_map/pallas_call | solution.py:152
  163.6 0.3 constant_dynamic-slice_fusion.1
  163.9 1.3 collective-permute-start.6
  165.2 0.2 collective-permute-start.7
  165.4 17.5 %collective-permute-done.6.refs_1_ = bf16[128,4096]{1,0:T(8,128)(2,1)S(1)} collective-permute-done((bf16[128,4096]{1,0:T(8,128)(2,1)S(1)}, bf16[128,4096]{1,0:T(8,128)(2,1)S(1)}, u32[]{:S(2)}, u32[]{:S(2)}) %collective-permute-start.6) | collective-permute-done | bytes 1048608 | tf_op jit(solution)/shard_map/ppermute | solution.py:194
  182.9 8.2 %copy-done.3 = f32[24584,2,128]{2,1,0:T(2,128)S(1)} copy-done((f32[24584,2,128]{2,1,0:T(2,128)S(1)}, f32[24584,2,128]{2,1,0:T(2,128)}, u32[]{:S(2)}) %copy-start.3) | copy-done | bytes 25174040
  191.1 46.4 %shard_map.147 = (bf16[128,4096]{1,0:T(8,128)(2,1)S(1)}, bf16[128,4096]{1,0:T(8,128)(2,1)S(1)}) custom-call(s32[1]{0:T(128)S(6)} %sub.17.live, s32[4,4096]{1,0:T(4,128)S(1)} %get-tuple-element.24.slots, bf16[128,4096]{1,0:T(8,128)(2,1)S(1)} %get-tuple-element.19.refs_0_, bf16[128,4096]{1,0:T(8,128)(2,1)S(1)} %collective-permute-done.6.refs_1_, ...), custom_call_target="tpu_custom_call" | custom-call | flops 2867200000 | bytes 8388608 | tf_op jit(solution)/shard_map/pallas_call | solution.py:152
  237.5 1.3 collective-permute-start.8
  238.8 0.1 constant_dynamic-update-slice_fusion.2
  238.9 0.0 collective-permute-done.7
  238.9 0.1 constant_dynamic-update-slice_fusion.1
  239.1 0.0 copy-start.12
  239.1 12.1 %collective-permute-done.8 = bf16[128,4096]{1,0:T(8,128)(2,1)S(1)} collective-permute-done((bf16[128,4096]{1,0:T(8,128)(2,1)S(1)}, bf16[128,4096]{1,0:T(8,128)(2,1)S(1)}, u32[]{:S(2)}, u32[]{:S(2)}) %collective-permute-start.8) | collective-permute-done | bytes 1048608 | tf_op jit(solution)/shard_map/ppermute | solution.py:194
  251.2 1.1 constant_dynamic-update-slice_fusion
  (43 shorter events, 0.2 us)
Async XLA Ops:
  0.0 14.2 %copy-start = (f32[4,16384]{1,0:T(4,128)S(1)}, f32[4,16384]{1,0:T(4,128)}, u32[]{:S(2)}) copy-start(f32[4,16384]{1,0:T(4,128)} %param.18) | copy-start | bytes 786436
  0.0 4.8 %copy-start.4 = (bf16[128,8192]{1,0:T(8,128)(2,1)S(1)}, bf16[128,8192]{1,0:T(8,128)(2,1)}, u32[]{:S(2)}) copy-start(bf16[128,8192]{1,0:T(8,128)(2,1)} %refs_2_.1) | copy-start | bytes 6291460
  0.0 13.9 %copy-start.13 = (bf16[256,256]{1,0:T(8,128)(2,1)S(1)}, bf16[256,256]{1,0:T(8,128)(2,1)}, u32[]{:S(2)}) copy-start(bf16[256,256]{1,0:T(8,128)(2,1)} %param.25) | copy-start | bytes 393220
  0.0 13.5 %copy-start.19 = (f32[256]{0:T(256)S(1)}, f32[256]{0:T(256)}, u32[]{:S(2)}) copy-start(f32[256]{0:T(256)} %param.28) | copy-start | bytes 3076
  0.0 13.5 %copy-start.18 = (f32[256]{0:T(256)S(1)}, f32[256]{0:T(256)}, u32[]{:S(2)}) copy-start(f32[256]{0:T(256)} %param.29) | copy-start | bytes 3076
  4.8 12.2 %copy-start.20 = (f32[256]{0:T(256)S(1)}, f32[256]{0:T(256)}, u32[]{:S(2)}) copy-start(f32[256]{0:T(256)} %param.27) | copy-start | bytes 3076
  4.8 12.2 %copy-start.21 = (f32[256]{0:T(256)S(1)}, f32[256]{0:T(256)}, u32[]{:S(2)}) copy-start(f32[256]{0:T(256)} %param.26) | copy-start | bytes 3076
  4.8 12.2 %copy-start.14 = (bf16[256,256]{1,0:T(8,128)(2,1)S(1)}, bf16[256,256]{1,0:T(8,128)(2,1)}, u32[]{:S(2)}) copy-start(bf16[256,256]{1,0:T(8,128)(2,1)} %param.21) | copy-start | bytes 393220
  4.8 12.9 %copy-start.15 = (bf16[256,256]{1,0:T(8,128)(2,1)S(1)}, bf16[256,256]{1,0:T(8,128)(2,1)}, u32[]{:S(2)}) copy-start(bf16[256,256]{1,0:T(8,128)(2,1)} %param.23) | copy-start | bytes 393220
  4.8 12.9 %copy-start.16 = (bf16[256,256]{1,0:T(8,128)(2,1)S(1)}, bf16[256,256]{1,0:T(8,128)(2,1)}, u32[]{:S(2)}) copy-start(bf16[256,256]{1,0:T(8,128)(2,1)} %param.20) | copy-start | bytes 393220
  4.8 47.6 %collective-permute-start = (bf16[128,8192]{1,0:T(8,128)(2,1)S(1)}, bf16[128,8192]{1,0:T(8,128)(2,1)}, u32[]{:S(2)}, u32[]{:S(2)}) collective-permute-start(bf16[128,8192]{1,0:T(8,128)(2,1)S(1)} %copy-done.4), channel_id=1, source_target_pairs={{0,1},{1,0},{2,3},{3,2},{4,5},{5,4},{6,7},{7,6},{8,9},{9,8},{10,11... | collective-permute-start | bytes 6291464 | tf_op jit(solution)/shard_map/ppermute | solution.py:194
  6.9 67.2 %collective-permute-start.2 = (bf16[128,8192]{1,0:T(8,128)(2,1)S(1)}, bf16[128,8192]{1,0:T(8,128)(2,1)}, u32[]{:S(2)}, u32[]{:S(2)}) collective-permute-start(bf16[128,8192]{1,0:T(8,128)(2,1)S(1)} %copy-done.4), channel_id=1, source_target_pairs={{0,2},{2,4},{4,6},{6,8},{8,10},{10,12},{12,14},{14,16},{16,18},{18... | collective-permute-start | bytes 6291464 | tf_op jit(solution)/shard_map/ppermute | solution.py:198
  10.9 63.3 %collective-permute-start.4 = (bf16[128,8192]{1,0:T(8,128)(2,1)S(1)}, bf16[128,8192]{1,0:T(8,128)(2,1)}, u32[]{:S(2)}, u32[]{:S(2)}) collective-permute-start(bf16[128,8192]{1,0:T(8,128)(2,1)S(1)} %copy-done.4), channel_id=1, source_target_pairs={{2,0},{4,2},{6,4},{8,6},{10,8},{12,10},{14,12},{16,14},{18,16},{20... | collective-permute-start | bytes 6291464 | tf_op jit(solution)/shard_map/ppermute | solution.py:199
  52.4 28.7 %collective-permute-start.5 = (bf16[128,8192]{1,0:T(8,128)(2,1)}, bf16[128,8192]{1,0:T(8,128)(2,1)}, u32[]{:S(2)}, u32[]{:S(2)}) collective-permute-start(bf16[128,8192]{1,0:T(8,128)(2,1)} %collective-permute-done.refs_3_), channel_id=1, source_target_pairs={{2,0},{4,2},{6,4},{8,6},{10,8},{12,10},{14,12},{16,14},{18,16},{20... | collective-permute-start | bytes 6291464 | tf_op jit(solution)/shard_map/ppermute | solution.py:199
  55.5 47.2 %collective-permute-start.3 = (bf16[128,8192]{1,0:T(8,128)(2,1)}, bf16[128,8192]{1,0:T(8,128)(2,1)}, u32[]{:S(2)}, u32[]{:S(2)}) collective-permute-start(bf16[128,8192]{1,0:T(8,128)(2,1)} %collective-permute-done.refs_3_), channel_id=1, source_target_pairs={{0,2},{2,4},{4,6},{6,8},{8,10},{10,12},{12,14},{14,16},{16,18},{18... | collective-permute-start | bytes 6291464 | tf_op jit(solution)/shard_map/ppermute | solution.py:198
  65.5 5.6 %copy-start.17 = (s32[4,16384]{1,0:T(4,128)S(1)}, s32[4,16384]{1,0:T(4,128)}, u32[]{:S(2)}) copy-start(s32[4,16384]{1,0:T(4,128)} %param.17) | copy-start | bytes 786436
  72.8 43.2 %collective-permute-start.1 = (bf16[128,4096]{1,0:T(8,128)(2,1)S(1)}, bf16[128,4096]{1,0:T(8,128)(2,1)S(1)}, u32[]{:S(2)}, u32[]{:S(2)}) collective-permute-start(bf16[128,4096]{1,0:T(8,128)(2,1)S(1)} %get-tuple-element.11), channel_id=1, source_target_pairs={{0,1},{1,0},{2,3},{3,2},{4,5},{5,4},{6,7},{7,6},{8,9},{9,8},{10,11... | collective-permute-start | bytes 3145736 | tf_op jit(solution)/shard_map/ppermute | solution.py:194
  74.1 41.9 %copy-start.6 = (bf16[256,256]{1,0:T(8,128)(2,1)S(1)}, bf16[256,256]{1,0:T(8,128)(2,1)}, u32[]{:S(2)}) copy-start(bf16[256,256]{1,0:T(8,128)(2,1)} %refs_5_.3) | copy-start | bytes 393220
  74.1 41.9 %copy-start.8 = (bf16[256,256]{1,0:T(8,128)(2,1)S(1)}, bf16[256,256]{1,0:T(8,128)(2,1)}, u32[]{:S(2)}) copy-start(bf16[256,256]{1,0:T(8,128)(2,1)} %refs_6_.3) | copy-start | bytes 393220
  102.7 1.6 copy-start.5
  104.3 0.9 copy-start.10
  116.0 47.5 %copy-start.2 = (f32[24584,2,128]{2,1,0:T(2,128)}, f32[24584,2,128]{2,1,0:T(2,128)S(1)}, u32[]{:S(2)}) copy-start(f32[24584,2,128]{2,1,0:T(2,128)S(1)} %shard_map.145.refs_2_) | copy-start | bytes 75522048
  116.1 47.5 %copy-start.11 = (bf16[128,16384]{1,0:T(8,128)(2,1)S(1)}, bf16[128,16384]{1,0:T(8,128)(2,1)}, u32[]{:S(2)}) copy-start(bf16[128,16384]{1,0:T(8,128)(2,1)} %copy.34) | copy-start | bytes 12582916
  163.5 19.4 %copy-start.7 = (bf16[256,256]{1,0:T(8,128)(2,1)S(1)}, bf16[256,256]{1,0:T(8,128)(2,1)}, u32[]{:S(2)}) copy-start(bf16[256,256]{1,0:T(8,128)(2,1)} %refs_5_.3) | copy-start | bytes 393220
  163.5 19.4 %copy-start.9 = (bf16[256,256]{1,0:T(8,128)(2,1)S(1)}, bf16[256,256]{1,0:T(8,128)(2,1)}, u32[]{:S(2)}) copy-start(bf16[256,256]{1,0:T(8,128)(2,1)} %refs_6_.3) | copy-start | bytes 393220
  163.9 19.0 %collective-permute-start.6 = (bf16[128,4096]{1,0:T(8,128)(2,1)S(1)}, bf16[128,4096]{1,0:T(8,128)(2,1)S(1)}, u32[]{:S(2)}, u32[]{:S(2)}) collective-permute-start(bf16[128,4096]{1,0:T(8,128)(2,1)S(1)} %get-tuple-element.13), channel_id=1, source_target_pairs={{0,1},{1,0},{2,3},{3,2},{4,5},{5,4},{6,7},{7,6},{8,9},{9,8},{10,11... | collective-permute-start | bytes 3145736 | tf_op jit(solution)/shard_map/ppermute | solution.py:194
  165.2 73.7 %collective-permute-start.7 = (bf16[128,4096]{1,0:T(8,128)(2,1)}, bf16[128,4096]{1,0:T(8,128)(2,1)S(1)}, u32[]{:S(2)}, u32[]{:S(2)}) collective-permute-start(bf16[128,4096]{1,0:T(8,128)(2,1)} %get-tuple-element.15), channel_id=1, source_target_pairs={{0,1},{1,0},{2,3},{3,2},{4,5},{5,4},{6,7},{7,6},{8,9},{9,8},{10,11... | collective-permute-start | bytes 3145736 | tf_op jit(solution)/shard_map/ppermute | solution.py:194
  182.9 8.2 %copy-start.3 = (f32[24584,2,128]{2,1,0:T(2,128)S(1)}, f32[24584,2,128]{2,1,0:T(2,128)}, u32[]{:S(2)}) copy-start(f32[24584,2,128]{2,1,0:T(2,128)} %copy-done.2) | copy-start | bytes 75522048
  191.1 61.2 %copy-start.1 = (f32[4,16384]{1,0:T(4,128)S(1)}, f32[4,16384]{1,0:T(4,128)}, u32[]{:S(2)}) copy-start(f32[4,16384]{1,0:T(4,128)} %param.18) | copy-start | bytes 786436
  237.5 13.7 %collective-permute-start.8 = (bf16[128,4096]{1,0:T(8,128)(2,1)S(1)}, bf16[128,4096]{1,0:T(8,128)(2,1)S(1)}, u32[]{:S(2)}, u32[]{:S(2)}) collective-permute-start(bf16[128,4096]{1,0:T(8,128)(2,1)S(1)} %get-tuple-element.16), channel_id=1, source_target_pairs={{0,1},{1,0},{2,3},{3,2},{4,5},{5,4},{6,7},{7,6},{8,9},{9,8},{10,11... | collective-permute-start | bytes 3145736 | tf_op jit(solution)/shard_map/ppermute | solution.py:194
  239.1 12.2 %copy-start.12 = (bf16[128,16384]{1,0:T(8,128)(2,1)}, bf16[128,16384]{1,0:T(8,128)(2,1)S(1)}, u32[]{:S(2)}) copy-start(bf16[128,16384]{1,0:T(8,128)(2,1)S(1)} %constant_dynamic-update-slice_fusion.1) | copy-start | bytes 12582916
